TPU v7x, 32 devices: a whole 2x2x4 slice. The times are simulated.
32 devices in a mesh: groups: 2 (over y), lat: 4 (over z), wid: 2 (over x), dat: 2 (over core).
Axes of the slice: x: 2, y: 2, z: 4, core: 2. Of those that a mesh axis runs over, the one named last changes fastest.
Arguments:
- inputs: bfloat16 [1024, 3584], P(('groups', 'dat'), 'wid'), parts along dimension 0, may hold values from -6 to 6
- weight: bfloat16 [16384, 3584], P(('groups', 'lat', 'dat'), 'wid'), parts along dimension 0, may hold values from -0.09375 to 0.09375
- enc_bias: float32 [16384], P(('groups', 'lat')), parts along dimension 0, may hold values from -3 to 3
- dec_bias: float32 [7168], P(('groups', 'wid')), parts along dimension 0, may hold values from -5 to 5
- row_code: int32 [1024], P('groups'), parts along dimension 0, may hold values from 1 to 4092
- lat_code: int32 [16384], P(('groups', 'lat')), parts along dimension 0, may hold values from 1 to 4092
- lat_thr: int32 [16384], P(('groups', 'lat')), parts along dimension 0, may hold values from 41 to 204
- loss_scale: float32 [1], replicated, may hold values from 8 to 32
Outputs:
- grad_weight: bfloat16 [16384, 3584], P(('groups', 'lat', 'dat'), 'wid'), parts along dimension 0
- grad_enc_bias: float32 [16384], P(('groups', 'lat')), parts along dimension 0
- grad_dec_bias: float32 [7168], P(('groups', 'wid')), parts along dimension 0
There are 2 independent parts, one for each index of `groups`. A program takes and returns all parts, laid end to end along the dimension named above; an argument that names none is the same for every part. Nothing has to cross between parts.
All inputs are finite; a program needn't handle non-finite values.
Results may differ from a plain program's by a relative error of at most 0.017.
Values may be sent and summed in bfloat16 or wider, within the bound.
A program may use at most 128 MiB of HBM per device.

v0:
```python
import jax
import jax.numpy as jnp
from jax import lax
from jax.sharding import PartitionSpec as P


def times_rows(left, right):
    return lax.dot_general(
        left, right, (((1,), (1,)), ((), ())), preferred_element_type=jnp.float32
    )


def columns_first(left, right):
    return lax.dot_general(
        left, right, (((0,), (0,)), ((), ())), preferred_element_type=jnp.float32
    )


def per_device(inputs, weight, enc_bias, dec_bias, row_code, lat_code, lat_thr, loss_scale):
    place = lax.axis_index("dat")
    lats = weight.shape[0]
    mine = lambda v: lax.dynamic_slice_in_dim(v, place * lats, lats, 0)
    rows = lax.all_gather(inputs, "dat", axis=0, tiled=True)
    total_rows = rows.shape[0]
    active = row_code[:, None] * mine(lat_code)[None, :] % 4093 < mine(lat_thr)[None, :]
    pre = (
        lax.psum(times_rows(rows, weight).astype(jnp.bfloat16), "wid").astype(jnp.float32)
        + mine(enc_bias)[None, :]
    )
    acts = jnp.where(active, pre, 0.0).astype(jnp.bfloat16)
    partial_value = jnp.dot(acts, weight, preferred_element_type=jnp.float32)
    recon = lax.psum(partial_value.astype(jnp.bfloat16), ("lat", "dat")).astype(jnp.float32)
    recon = recon + dec_bias[None, :]
    g_rec = loss_scale[0] * (2.0 / total_rows) * (recon - rows.astype(jnp.float32))
    g_bf = g_rec.astype(jnp.bfloat16)
    g_acts = lax.psum(times_rows(g_bf, weight).astype(jnp.bfloat16), "wid").astype(jnp.float32)
    g_pre = jnp.where(active, g_acts, 0.0).astype(jnp.bfloat16)
    grad_weight = (columns_first(acts, g_bf) + columns_first(g_pre, rows)).astype(jnp.bfloat16)
    latent_total = jnp.sum(g_pre.astype(jnp.float32), axis=0)
    grad_enc_bias = lax.all_gather(latent_total, "dat", axis=0, tiled=True)
    return (grad_weight, grad_enc_bias, jnp.sum(g_rec, axis=0))


def solution(mesh):
    return jax.shard_map(
        per_device,
        mesh=mesh,
        in_specs=(
            P(("groups", "dat"), "wid"),
            P(("groups", "lat", "dat"), "wid"),
            P(("groups", "lat")),
            P(("groups", "wid")),
            P("groups"),
            P(("groups", "lat")),
            P(("groups", "lat")),
            P(),
        ),
        out_specs=(P(("groups", "lat", "dat"), "wid"), P(("groups", "lat")), P(("groups", "wid"))),
        check_vma=False,
    )
```

profile of v0, /device:TPU:0, one launch (start us, length us, event | category | flops | bytes accessed | tf_op | source)
XLA Modules:
  0.0 205.0 jit_solution(18160524312689692306)
XLA Ops:
  7.2 0.0 all-gather.2.cloned.1.call-start
  7.2 0.7 all-gather.2.cloned.1.call-update
  7.9 0.0 copy-start.4
  7.9 0.0 copy-start.5
  7.9 0.0 copy-start.6
  7.9 0.0 copy-start.3
  7.9 0.0 all-reduce.4.cloned.1.call-start
  8.0 14.5 %all-gather.2.cloned.1.call-done = bf16[512,1792]{1,0:T(8,128)(2,1)} async-done(((bf16[256,1792]{1,0:T(8,128)(2,1)}), bf16[512,1792]{1,0:T(8,128)(2,1)}) %all-gather.2.cloned.1.call-update) | async-done | bytes 1835024 | tf_op jit(solution)/shard_map/all_gather | solution.py:23
  22.5 5.7 %convolution_convert_fusion.2 = bf16[512,1024]{1,0:T(8,128)(2,1)} fusion(bf16[512,1792]{1,0:T(8,128)(2,1)} %all-gather.2.cloned.1.call-done, bf16[1024,1792]{1,0:T(8,128)(2,1)} %param.9), kind=kOutput, calls=%fused_computation.15 | convolution fusion | flops 1879572480 | bytes 6553600 | tf_op jit(solution)/shard_map/dot_general | solution.py:8
  28.1 0.0 all-reduce.4.cloned.1.call-update
  28.1 0.0 all-reduce.6.cloned.1.call-start
  28.2 0.0 copy-done.4
  28.2 0.0 copy-done.5
  28.3 0.0 copy-done.6
  28.3 0.0 copy-start
  28.3 0.0 copy-start.2
  28.3 41.2 %all-reduce.4.cloned.1.call-done = bf16[512,1024]{1,0:T(8,128)(2,1)} async-done(((bf16[512,1024]{1,0:T(8,128)(2,1)}), bf16[512,1024]{1,0:T(8,128)(2,1)}) %all-reduce.4.cloned.1.call-update) | async-done | bytes 1048592 | tf_op jit(solution)/shard_map/psum | solution.py:27
  69.5 0.0 copy-done.3
  69.5 6.8 %convolution_convert_fusion = bf16[512,1792]{1,0:T(8,128)(2,1)} fusion(bf16[1024,1792]{1,0:T(8,128)(2,1)} %param.9, bf16[512,1024]{1,0:T(8,128)(2,1)} %all-reduce.4.cloned.1.call-done, f32[1024]{0:T(1024)S(1)} %dynamic_slice.11, s32[1024]{0:T(1024)S(1)} %dynamic_slice.10, s32[1024]{0:T(1024)S(1)} %dynamic_slice.9, s32[512]{0:T(512)S(1)} %copy-done.3), kind=kOutput, calls=%fused_computation.5 | convolution fusion | flops 1886257152 | bytes 6567936 | tf_op jit(solution)/shard_map/dot_general | solution.py:31
  76.3 0.0 all-reduce.6.cloned.1.call-update
  76.4 0.0 all-reduce.8.cloned.1.call-start
  77.1 62.6 %all-reduce.6.cloned.1.call-done = bf16[512,1792]{1,0:T(8,128)(2,1)} async-done(((bf16[512,1792]{1,0:T(8,128)(2,1)}), bf16[512,1792]{1,0:T(8,128)(2,1)}) %all-reduce.6.cloned.1.call-update) | async-done | bytes 1835024 | tf_op jit(solution)/shard_map/psum | solution.py:32
  139.7 5.7 %convolution_convert_fusion.1 = bf16[512,1024]{1,0:T(8,128)(2,1)} fusion(bf16[1024,1792]{1,0:T(8,128)(2,1)} %param.9, bf16[512,1792]{1,0:T(8,128)(2,1)S(1)} %copy-done, bf16[512,1792]{1,0:T(8,128)(2,1)} %all-reduce.6.cloned.1.call-done, f32[1792]{0:T(1024)S(1)} %copy-done.2, f32[]{:T(128)} %bitcast), kind=kOutput, calls=%fused_computation.14 | convolution fusion | flops 1885077504 | bytes 8395780 | tf_op jit(solution)/shard_map/dot_general | solution.py:8
  145.4 0.0 all-reduce.8.cloned.1.call-update
  145.4 3.0 %fusion = f32[1792]{0:T(1024)} fusion(bf16[512,1792]{1,0:T(8,128)(2,1)S(1)} %copy-done, bf16[512,1792]{1,0:T(8,128)(2,1)} %all-reduce.6.cloned.1.call-done, f32[1792]{0:T(1024)S(1)} %copy-done.2, f32[]{:T(128)} %bitcast), kind=kLoop, calls=%fused_computation.3 | loop fusion | flops 5503232 | bytes 3684356 | tf_op jit(solution)/shard_map/reduce_sum | solution.py:41
  148.4 0.0 copy-done.7
  148.4 6.3 %fusion.6 = f32[1024,1792]{1,0:T(8,128)} fusion(bf16[512,1024]{1,0:T(8,128)(2,1)S(1)} %copy-done.7, f32[1024]{0:T(1024)S(1)} %dynamic_slice.11, s32[1024]{0:T(1024)S(1)} %dynamic_slice.10, s32[1024]{0:T(1024)S(1)} %dynamic_slice.9, s32[512]{0:T(512)S(1)} %copy-done.3, bf16[512,1792]{1,0:T(8,128)(2,1)S(1)} %copy-done, bf16[512,1792]{1,0:T(8,128)(2,1)S(1)} %copy-done.1, ...), kind=kOutput, calls=%fused_computation.16 | convolution fusion | flops 1890844672 | bytes 12080132 | tf_op jit(solution)/shard_map/dot_general | solution.py:14
  154.7 30.3 %all-reduce.8.cloned.1.call-done = bf16[512,1024]{1,0:T(8,128)(2,1)} async-done(((bf16[512,1024]{1,0:T(8,128)(2,1)}), bf16[512,1024]{1,0:T(8,128)(2,1)}) %all-reduce.8.cloned.1.call-update) | async-done | bytes 1048592 | tf_op jit(solution)/shard_map/psum | solution.py:36
  185.0 2.6 %convert_reduce_fusion = f32[1024]{0:T(1024)S(1)} fusion(bf16[512,1024]{1,0:T(8,128)(2,1)} %all-reduce.8.cloned.1.call-done, s32[1024]{0:T(1024)S(1)} %dynamic_slice.10, s32[1024]{0:T(1024)S(1)} %dynamic_slice.9, s32[512]{0:T(512)S(1)} %copy-done.3), kind=kLoop, calls=%fused_computation.7 | loop fusion | flops 6814720 | bytes 1062912 | tf_op jit(solution)/shard_map/reduce_sum | solution.py:39
  187.6 2.0 all_gather.7
  189.6 8.3 %add_convert_fusion = bf16[1024,1792]{1,0:T(8,128)(2,1)} fusion(f32[1024,1792]{1,0:T(8,128)} %fusion.6, bf16[512,1792]{1,0:T(8,128)(2,1)S(1)} %copy-done, bf16[512,1024]{1,0:T(8,128)(2,1)} %all-reduce.8.cloned.1.call-done, s32[1024]{0:T(1024)S(1)} %dynamic_slice.10, s32[1024]{0:T(1024)S(1)} %dynamic_slice.9, s32[512]{0:T(512)S(1)} %copy-done.3), kind=kOutput, calls=%fused_computation | convolution fusion | flops 1888485376 | bytes 13903872 | tf_op jit(solution)/shard_map/dot_general | solution.py:14
  197.9 0.6 copy.16
  (8 shorter events, 0.0 us)
Async XLA Ops:
  7.2 15.3 %all-gather.2.cloned.1.call-start = ((), (), s32[]{:S(2)}) async-start(), calls=%async_computation | async-start | bytes 2752512 | tf_op jit(solution)/shard_map/all_gather | solution.py:23
  7.9 20.3 %copy-start.4 = (s32[2048]{0:T(1024)S(1)}, s32[2048]{0:T(1024)}, u32[]{:S(2)}) copy-start(s32[2048]{0:T(1024)} %param.13) | copy-start | bytes 24580
  7.9 20.3 %copy-start.5 = (s32[2048]{0:T(1024)S(1)}, s32[2048]{0:T(1024)}, u32[]{:S(2)}) copy-start(s32[2048]{0:T(1024)} %param.14) | copy-start | bytes 24580
  7.9 20.3 %copy-start.6 = (f32[2048]{0:T(1024)S(1)}, f32[2048]{0:T(1024)}, u32[]{:S(2)}) copy-start(f32[2048]{0:T(1024)} %param.10) | copy-start | bytes 24580
  7.9 61.6 %copy-start.3 = (s32[512]{0:T(512)S(1)}, s32[512]{0:T(512)}, u32[]{:S(2)}) copy-start(s32[512]{0:T(512)} %param.12) | copy-start | bytes 6148
  7.9 61.6 %all-reduce.4.cloned.1.call-start = ((), (), s32[]{:S(2)}) async-start(), calls=%async_computation.1 | async-start | bytes 2097152 | tf_op jit(solution)/shard_map/psum | solution.py:27
  28.1 111.5 %all-reduce.6.cloned.1.call-start = ((), (), s32[]{:S(2)}) async-start(), calls=%async_computation.2 | async-start | bytes 3670016 | tf_op jit(solution)/shard_map/psum | solution.py:32
  28.3 111.4 %copy-start = (bf16[512,1792]{1,0:T(8,128)(2,1)S(1)}, bf16[512,1792]{1,0:T(8,128)(2,1)}, u32[]{:S(2)}) copy-start(bf16[512,1792]{1,0:T(8,128)(2,1)} %all-gather.2.cloned.1.call-done) | copy-start | bytes 5505028
  28.3 111.4 %copy-start.2 = (f32[1792]{0:T(1024)S(1)}, f32[1792]{0:T(1024)}, u32[]{:S(2)}) copy-start(f32[1792]{0:T(1024)} %param.11) | copy-start | bytes 21508
  76.4 108.7 %all-reduce.8.cloned.1.call-start = ((), (), s32[]{:S(2)}) async-start(), calls=%async_computation.3 | async-start | bytes 2097152 | tf_op jit(solution)/shard_map/psum | solution.py:36
  145.4 3.0 %copy-start.1 = (bf16[512,1792]{1,0:T(8,128)(2,1)S(1)}, bf16[512,1792]{1,0:T(8,128)(2,1)}, u32[]{:S(2)}) copy-start(bf16[512,1792]{1,0:T(8,128)(2,1)} %all-reduce.6.cloned.1.call-done) | copy-start | bytes 5505028
  145.4 3.0 %copy-start.7 = (bf16[512,1024]{1,0:T(8,128)(2,1)S(1)}, bf16[512,1024]{1,0:T(8,128)(2,1)}, u32[]{:S(2)}) copy-start(bf16[512,1024]{1,0:T(8,128)(2,1)} %all-reduce.4.cloned.1.call-done) | copy-start | bytes 3145732
Sparse Core Ops, SparseCore 0:
  9.5 12.8 all-gather.1
  28.3 41.1 all-reduce.3
  76.5 63.1 all-reduce.5
  145.5 39.4 all-reduce.7
where the time goes:
time: 205 us
  waiting for transfers between devices  149 us (73%)
  matrix products  32.8 us (16%)
  between operations  14.5 us (7%)
  other arithmetic  5.56 us (3%)
    psum x1, waiting for transfers between devices, per_device(): lax.psum(partial_value.astype(jnp.bfloat16), ('lat', 'dat'))  62.6 us
    psum x1, waiting for transfers between devices, per_device(): lax.psum(times_rows(rows, weight).astype(jnp.bfloat16), 'wid')  41.2 us
    psum x1, waiting for transfers between devices, per_device(): lax.psum(times_rows(g_bf, weight).astype(jnp.bfloat16), 'wid')  30.3 us
    dot_general x2, matrix products, columns_first(): lax.dot_general(left, right, (((0,), (0,)), ((), ())), preferred_element_...  14.7 us
    all_gather x1, waiting for transfers between devices, per_device(): rows = lax.all_gather(inputs, 'dat', axis=0, tiled=True)  14.5 us
    dot_general x2, matrix products, times_rows(): lax.dot_general(left, right, (((1,), (1,)), ((), ())), preferred_element_...  11.3 us
    dot_general x1, matrix products, per_device(): partial_value = jnp.dot(acts, weight, preferred_element_type=jnp.float32)  6.83 us
  transfers between devices with their start and end apart: 4, of which 4 were waited for; matrix products, arithmetic and copies ran while one was open for 5% of the time, Pallas kernels for 0%

commit v1 on v0

--- a/solution.py
+++ b/solution.py
@@ -1,7 +1,19 @@
+import functools
+
 import jax
 import jax.numpy as jnp
 from jax import lax
+from jax.experimental import pallas as pl
+from jax.experimental.pallas import tpu as pltpu
 from jax.sharding import PartitionSpec as P
+
+MESH = pl.DeviceIdType.MESH
+BF16 = jnp.bfloat16
+F32 = jnp.float32
+CHUNKS = 4
+TILE = 256
+STAGE_AT = (0, 10, 15, 22, 29, 32, 40)
+CHUNK_STEP = 8
 
 
 def times_rows(left, right):
@@ -41,9 +53,224 @@
     return (grad_weight, grad_enc_bias, jnp.sum(g_rec, axis=0))
 
 
+def kernel(
+    n_wid, n_lat, scale_ref, x_ref, w_ref, eb_ref, db_ref, rc_ref, lc_ref, thr_ref,
+    gw_ref, ge_ref, gd_ref,
+    x_all, p_out, p_in, acts_t, rec, rec_in, summed, pieces, g_all, q_out, q_in, g_pre_t, grad, eb_sum,
+    x_sem, p_sem, c_sem, s_sem, a_sem, h_sem, q_sem, e_sem,
+):
+    wid, lat, dat = lax.axis_index("wid"), lax.axis_index("lat"), lax.axis_index("dat")
+    other = 1 - dat
+    half, width = x_all.shape[2:]
+    lats = w_ref.shape[0]
+    rows = 2 * half
+    wid_peers = [lax.rem(wid + k, n_wid) for k in range(1, n_wid)]
+    lat_peers = [lax.rem(lat + k, n_lat) for k in range(1, n_lat)]
+
+    barrier = pltpu.get_barrier_semaphore()
+    everyone = [{"dat": other}] + [{"wid": p} for p in wid_peers] + [{"lat": p} for p in lat_peers]
+    for peer in everyone:
+        pl.semaphore_signal(barrier, inc=1, device_id=peer, device_id_type=MESH)
+    pl.semaphore_wait(barrier, len(everyone))
+
+    def copy(src, dst, sems, peer):
+        return pltpu.make_async_remote_copy(
+            src_ref=src, dst_ref=dst, send_sem=sems.at[0], recv_sem=sems.at[1],
+            device_id=peer, device_id_type=MESH,
+        )
+
+    def x_copy(c):
+        return copy(x_ref.at[c], x_all.at[c, dat], x_sem.at[c], {"dat": other})
+
+    def p_copies(c):
+        return [copy(p_out.at[c], p_in.at[c, k], p_sem.at[c, k], {"wid": p}) for k, p in enumerate(wid_peers)]
+
+    def q_copies(c):
+        return [copy(q_out.at[c], q_in.at[c, k], q_sem.at[c, k], {"wid": p}) for k, p in enumerate(wid_peers)]
+
+    def c_copy(c):
+        return copy(rec.at[c, other], rec_in.at[c], c_sem.at[c], {"dat": other})
+
+    def s_copies(c):
+        return [copy(summed.at[c, p], pieces.at[c, k], s_sem.at[c, k], {"lat": p}) for k, p in enumerate(lat_peers)]
+
+    def a_copies(c):
+        return [
+            copy(g_all.at[c, dat, lat], g_all.at[c, dat, lat], a_sem.at[c, k], {"lat": p})
+            for k, p in enumerate(lat_peers)
+        ]
+
+    def h_copy(c):
+        return copy(g_all.at[c, dat], g_all.at[c, dat], h_sem.at[c], {"dat": other})
+
+    def active(c):
+        product = rc_ref[c].astype(F32) * lc_ref[dat].astype(F32)
+        left = product - jnp.floor(product * (1.0 / 4093.0)) * 4093.0
+        left = jnp.where(left < 0.0, left + 4093.0, left)
+        left = jnp.where(left >= 4093.0, left - 4093.0, left)
+        return left < thr_ref[dat].astype(F32)
+
+    def by_latents(value, out, c):
+        for t in range(lats // TILE):
+            cols = slice(t * TILE, (t + 1) * TILE)
+            out[c, :, cols] = times_rows(value, w_ref[cols, :]).astype(BF16)
+
+    def total(out, into, c):
+        value = out[c].astype(F32)
+        for k in range(n_wid - 1):
+            value = value + into[c, k].astype(F32)
+        return value
+
+    def encode(c):
+        x_copy(c).wait()
+        by_latents(x_all[c].reshape(rows, width), p_out, c)
+        for one in p_copies(c):
+            one.start()
+
+    def decode(c):
+        for one in p_copies(c):
+            one.wait()
+        acts = jnp.where(active(c), total(p_out, p_in, c) + eb_ref[dat], 0.0)
+        acts_t[:, c * rows:(c + 1) * rows] = acts.T.astype(BF16)
+        acts = acts.astype(BF16)
+        for t in range(width // TILE):
+            cols = slice(t * TILE, (t + 1) * TILE)
+            part = jnp.dot(acts, w_ref[:, cols], preferred_element_type=F32)
+            rec[c, :, :, cols] = part.astype(BF16).reshape(2, half, TILE)
+        c_copy(c).start()
+
+    def core_sum(c):
+        c_copy(c).wait()
+        both = rec[c, dat].astype(F32) + rec_in[c].astype(F32)
+        summed[c] = both.astype(BF16).reshape(summed.shape[1:])
+        for one in s_copies(c):
+            one.start()
+
+    def gradient(c):
+        for one in s_copies(c):
+            one.wait()
+        recon = summed[c, lat].astype(F32)
+        for k in range(n_lat - 1):
+            recon = recon + pieces[c, k].astype(F32)
+        own = x_piece(c)
+        g_rec = scale_ref[0] * (2.0 / (rows * CHUNKS)) * (recon + db_ref[...] - own.astype(F32))
+        g_all[c, dat, lat] = g_rec.astype(BF16)
+        for one in a_copies(c):
+            one.start()
+
+    def x_piece(c):
+        count = half // n_lat
+        return x_ref[c, pl.ds(pl.multiple_of(lat * count, count), count), :]
+
+    def share(c):
+        for one in a_copies(c):
+            one.wait()
+        h_copy(c).start()
+
+    def back(c):
+        h_copy(c).wait()
+        g_rows = g_all[c].reshape(rows, width)
+        column = jnp.sum(g_rows.astype(F32), axis=0, keepdims=True)
+        gd_ref[...] = column if c == 0 else gd_ref[...] + column
+        by_latents(g_rows, q_out, c)
+        for one in q_copies(c):
+            one.start()
+
+    def gate(c):
+        for one in q_copies(c):
+            one.wait()
+        g_pre = jnp.where(active(c), total(q_out, q_in, c), 0.0).astype(BF16).astype(F32)
+        g_pre_t[:, c * rows:(c + 1) * rows] = g_pre.T.astype(BF16)
+        column = jnp.sum(g_pre, axis=0, keepdims=True)
+        eb_sum[dat] = column if c == 0 else eb_sum[dat] + column
+
+    for c in range(CHUNKS):
+        x_copy(c).start()
+    x_all[:, dat] = x_ref[...]
+    stages = (encode, decode, core_sum, gradient, share, back, gate)
+    order = sorted(
+        (STAGE_AT[s] + (CHUNK_STEP if s else 1) * c, s, c) for s in range(len(stages)) for c in range(CHUNKS)
+    )
+    for _, s, c in order:
+        if s == len(stages) - 1 and c == CHUNKS - 1:
+            for t in range(width // TILE):
+                cols = slice(t * TILE, (t + 1) * TILE)
+                right = g_all[:, :, :, :, cols].reshape(CHUNKS * rows, TILE)
+                grad[:, cols] = jnp.dot(acts_t[...], right, preferred_element_type=F32)
+        stages[s](c)
+    e_copy = copy(eb_sum.at[dat], eb_sum.at[dat], e_sem, {"dat": other})
+    e_copy.start()
+    for t in range(width // TILE):
+        cols = slice(t * TILE, (t + 1) * TILE)
+        right = x_all[:, :, :, cols].reshape(CHUNKS * rows, TILE)
+        grown = grad[:, cols] + jnp.dot(g_pre_t[...], right, preferred_element_type=F32)
+        gw_ref[:, cols] = grown.astype(BF16)
+    e_copy.wait()
+    ge_ref[...] = eb_sum[...]
+
+
+def fused(n_wid, n_lat, inputs, weight, enc_bias, dec_bias, row_code, lat_code, lat_thr, loss_scale):
+    lats, width = weight.shape
+    half = inputs.shape[0] // CHUNKS
+    rows, piece = 2 * half, half // n_lat
+    whole = pl.BlockSpec(memory_space=pltpu.VMEM)
+    codes = jnp.swapaxes(row_code.reshape(2, CHUNKS, half), 0, 1).reshape(CHUNKS, rows, 1)
+    pair = lambda v: v.reshape(2, 1, lats)
+    sems = lambda *shape: pltpu.SemaphoreType.DMA(shape + (2,))
+    grad_weight, grad_enc_bias, grad_dec_bias = pl.pallas_call(
+        functools.partial(kernel, n_wid, n_lat),
+        out_shape=(
+            jax.ShapeDtypeStruct((lats, width), BF16),
+            jax.ShapeDtypeStruct((2, 1, lats), F32),
+            jax.ShapeDtypeStruct((1, width), F32),
+        ),
+        in_specs=[pl.BlockSpec(memory_space=pltpu.SMEM)] + [whole] * 7,
+        out_specs=(whole,) * 3,
+        scratch_shapes=[
+            pltpu.VMEM((CHUNKS, 2, half, width), BF16),
+            pltpu.VMEM((CHUNKS, rows, lats), BF16),
+            pltpu.VMEM((CHUNKS, n_wid - 1, rows, lats), BF16),
+            pltpu.VMEM((lats, CHUNKS * rows), BF16),
+            pltpu.VMEM((CHUNKS, 2, half, width), BF16),
+            pltpu.VMEM((CHUNKS, half, width), BF16),
+            pltpu.VMEM((CHUNKS, n_lat, piece, width), BF16),
+            pltpu.VMEM((CHUNKS, n_lat - 1, piece, width), BF16),
+            pltpu.VMEM((CHUNKS, 2, n_lat, piece, width), BF16),
+            pltpu.VMEM((CHUNKS, rows, lats), BF16),
+            pltpu.VMEM((CHUNKS, n_wid - 1, rows, lats), BF16),
+            pltpu.VMEM((lats, CHUNKS * rows), BF16),
+            pltpu.VMEM((lats, width), F32),
+            pltpu.VMEM((2, 1, lats), F32),
+            sems(CHUNKS), sems(CHUNKS, n_wid - 1), sems(CHUNKS), sems(CHUNKS, n_lat - 1),
+            sems(CHUNKS, n_lat - 1), sems(CHUNKS), sems(CHUNKS, n_wid - 1), sems(),
+        ],
+        compiler_params=pltpu.CompilerParams(
+            collective_id=0, has_side_effects=True, vmem_limit_bytes=56 * 1024 * 1024
+        ),
+    )(
+        loss_scale, inputs.reshape(CHUNKS, half, width), weight, pair(enc_bias),
+        dec_bias.reshape(1, width), codes, pair(lat_code), pair(lat_thr),
+    )
+    return (grad_weight, grad_enc_bias.reshape(-1), grad_dec_bias.reshape(-1))
+
+
+def fits(mesh, rows, lats, width):
+    n_wid, n_lat = mesh.shape["wid"], mesh.shape["lat"]
+    return (
+        mesh.shape["dat"] == 2 and n_wid == 2 and 2 <= n_lat <= 8
+        and rows % (CHUNKS * n_lat * 16) == 0 and lats % TILE == 0 and width % TILE == 0
+        and lats * width <= 2 ** 21 and rows <= 256
+    )
+
+
 def solution(mesh):
+    def body(inputs, weight, *rest):
+        if fits(mesh, inputs.shape[0], weight.shape[0], weight.shape[1]):
+            return fused(mesh.shape["wid"], mesh.shape["lat"], inputs, weight, *rest)
+        return per_device(inputs, weight, *rest)
+
     return jax.shard_map(
-        per_device,
+        body,
         mesh=mesh,
         in_specs=(
             P(("groups", "dat"), "wid"),

time: 205 us -> 92.1 us (0.45)
  waiting for transfers between devices: 149 us -> 0 us
  Pallas kernels: 0 us -> 81.5 us
  matrix products: 32.8 us -> 0 us
  between operations: 14.5 us -> 1.29 us
  local copies, waits for them, and re-layouts: 0.66 us -> 7.7 us
  other arithmetic: 5.56 us -> 1.31 us
    psum x3 -> x0, waiting for transfers between devices: 134 us -> none  [the longest x1 62.6 us: per_device(): lax.psum(partial_value.astype(jnp.bfloat16), ('lat', 'dat'))]
    pallas_call x0 -> x1, Pallas kernels: none -> 81.5 us  [fused(): pl.pallas_call(functools.partial(kernel, n_wid, n_lat), out_shape=(jax.Sh...]
    dot_general x5 -> x0, matrix products: 32.8 us -> none  [the longest x2 14.7 us: columns_first(): lax.dot_general(left, right, (((0,), (0,)), ((), ())), preferred_element_...]
    all_gather x1 -> x0, waiting for transfers between devices: 14.5 us -> none  [per_device(): rows = lax.all_gather(inputs, 'dat', axis=0, tiled=True)]
    reduce_sum x2 -> x0, other arithmetic: 5.56 us -> none  [the longest x1 2.98 us: per_device(): return (grad_weight, grad_enc_bias, jnp.sum(g_rec, axis=0))]
    unnamed x17 -> x4, local copies, waits for them, and re-layouts: 0.63 us -> 4.73 us
    reshape x0 -> x3, local copies, waits for them, and re-layouts: none -> 2.97 us  [the longest x1 1.29 us: fused(): dec_bias.reshape(1, width)]
  transfers between devices with their start and end apart: 4 -> 0, of which waited for: 4 -> 0; matrix products, arithmetic and copies ran while one was open for 5% -> 0% of each run, Pallas kernels for 0% -> 0%
where the time goes in v1:
time: 92.1 us; the launch traced here: 91.8 us
  Pallas kernels  81.5 us (88%)
  local copies, waits for them, and re-layouts  7.7 us (8%)
  other arithmetic  1.31 us (1%)
  between operations  1.29 us (1%)
    pallas_call x1, Pallas kernels, fused(): pl.pallas_call(functools.partial(kernel, n_wid, n_lat), out_shape=(jax.Sh...  81.5 us
    unnamed x4, local copies, waits for them, and re-layouts  4.73 us

profile of v1, /device:TPU:0, one launch (start us, length us, event | category | flops | bytes accessed | tf_op | source)
XLA Modules:
  0.0 91.8 jit_solution(11905493409016867837)
XLA Ops:
  1.3 0.8 reshape.36
  2.0 1.3 %reshape.35.db_ref = f32[1,1792]{1,0:T(1,128)} reshape(f32[1792]{0:T(1024)} %param.11) | data formatting | bytes 14336 | tf_op jit(solution)/shard_map/reshape | solution.py:252
  3.3 0.9 reshape.42.rc_ref
  4.3 81.5 %shard_map.103 = (bf16[1024,1792]{1,0:T(8,128)(2,1)}, f32[2,1,1024]{2,1,0:T(1,128)}, f32[1,1792]{1,0:T(1,128)}) custom-call(f32[1]{0:T(128)S(6)} %copy.15.scale_ref, bf16[4,64,1792]{2,1,0:T(8,128)(2,1)} %bitcast.6, bf16[1024,1792]{1,0:T(8,128)(2,1)} %w_ref.1, f32[2,1,1024]{2,1,0:T(1,128)} %bitcast.8, f32[1,1792]{1,0:T(1,128)} %reshape.35.db_ref, ...), custom_call_target="tpu_custom_call" | custom-call | tf_op jit(solution)/shard_map/pallas_call | solution.py:220
  85.8 1.3 %reduce = f32[1792]{0:T(1024)} reduce(f32[1,1792]{1,0:T(1,128)} %get-tuple-element.8, f32[]{:T(128)} %constant), dimensions={0}, to_apply=%get-tuple-element.8.reduce_sub_computation | reduce | bytes 14340 | tf_op jit(solution)/shard_map/pallas_call | solution.py:220
  87.1 0.0 copy-start
  87.1 4.1 %copy.16 = bf16[1024,1792]{1,0:T(8,128)(2,1)} copy(bf16[1024,1792]{1,0:T(8,128)(2,1)} %get-tuple-element.12) | data formatting | bytes 7340032
  91.2 0.0 copy-done
  91.2 0.6 copy.17
  (1 shorter events, 0.0 us)
Async XLA Ops:
  87.1 4.1 %copy-start = (f32[2,1,1024]{2,1,0:T(1,128)S(1)}, f32[2,1,1024]{2,1,0:T(1,128)}, u32[]{:S(2)}) copy-start(f32[2,1,1024]{2,1,0:T(1,128)} %get-tuple-element.7) | copy-start | bytes 24580

commit v2 on v1

--- a/solution.py
+++ b/solution.py
@@ -12,8 +12,9 @@
 F32 = jnp.float32
 CHUNKS = 4
 TILE = 256
-STAGE_AT = (0, 10, 15, 22, 29, 32, 40)
-CHUNK_STEP = 8
+LANES = 128
+STAGE_AT = (0, 10, 15, 30, 45, 48, 60)
+CHUNK_STEP = 10
 
 
 def times_rows(left, right):
@@ -56,8 +57,8 @@
 def kernel(
     n_wid, n_lat, scale_ref, x_ref, w_ref, eb_ref, db_ref, rc_ref, lc_ref, thr_ref,
     gw_ref, ge_ref, gd_ref,
-    x_all, p_out, p_in, acts_t, rec, rec_in, summed, pieces, g_all, q_out, q_in, g_pre_t, grad, eb_sum,
-    x_sem, p_sem, c_sem, s_sem, a_sem, h_sem, q_sem, e_sem,
+    x_all, p_out, p_in, acts_t, rec, rec_in, summed, pieces, g_all, q_out, q_in, g_pre_t, grad, done, eb_sum,
+    x_sem, p_sem, c_sem, s_sem, a_sem, h_sem, q_sem, e_sem, w_sem,
 ):
     wid, lat, dat = lax.axis_index("wid"), lax.axis_index("lat"), lax.axis_index("dat")
     other = 1 - dat
@@ -103,8 +104,14 @@
     def h_copy(c):
         return copy(g_all.at[c, dat], g_all.at[c, dat], h_sem.at[c], {"dat": other})
 
+    def row_codes(c):
+        line = rc_ref[...].astype(F32)
+        starts = (c * half, (CHUNKS + c) * half)
+        line = jnp.concatenate([line[:, at:at + half] for at in starts], axis=1)
+        return jnp.broadcast_to(line, (LANES, rows)).T[:, :1]
+
     def active(c):
-        product = rc_ref[c].astype(F32) * lc_ref[dat].astype(F32)
+        product = row_codes(c) * lc_ref[dat].astype(F32)
         left = product - jnp.floor(product * (1.0 / 4093.0)) * 4093.0
         left = jnp.where(left < 0.0, left + 4093.0, left)
         left = jnp.where(left >= 4093.0, left - 4093.0, left)
@@ -153,10 +160,13 @@
         for k in range(n_lat - 1):
             recon = recon + pieces[c, k].astype(F32)
         own = x_piece(c)
-        g_rec = scale_ref[0] * (2.0 / (rows * CHUNKS)) * (recon + db_ref[...] - own.astype(F32))
+        g_rec = scale_ref[0] * (2.0 / (rows * CHUNKS)) * (recon + bias_row() - own.astype(F32))
         g_all[c, dat, lat] = g_rec.astype(BF16)
         for one in a_copies(c):
             one.start()
+
+    def bias_row():
+        return jnp.concatenate([db_ref[i:i + 1, :] for i in range(width // LANES)], axis=1)
 
     def x_piece(c):
         count = half // n_lat
@@ -171,7 +181,9 @@
         h_copy(c).wait()
         g_rows = g_all[c].reshape(rows, width)
         column = jnp.sum(g_rows.astype(F32), axis=0, keepdims=True)
-        gd_ref[...] = column if c == 0 else gd_ref[...] + column
+        for i in range(width // LANES):
+            cell = column[:, i * LANES:(i + 1) * LANES]
+            gd_ref[i:i + 1, :] = cell if c == 0 else gd_ref[i:i + 1, :] + cell
         by_latents(g_rows, q_out, c)
         for one in q_copies(c):
             one.start()
@@ -184,6 +196,10 @@
         column = jnp.sum(g_pre, axis=0, keepdims=True)
         eb_sum[dat] = column if c == 0 else eb_sum[dat] + column
 
+    def out_copy(t):
+        cols = slice(t * TILE, (t + 1) * TILE)
+        return pltpu.make_async_copy(done.at[:, cols], gw_ref.at[:, cols], w_sem.at[t])
+
     for c in range(CHUNKS):
         x_copy(c).start()
     x_all[:, dat] = x_ref[...]
@@ -196,15 +212,21 @@
             for t in range(width // TILE):
                 cols = slice(t * TILE, (t + 1) * TILE)
                 right = g_all[:, :, :, :, cols].reshape(CHUNKS * rows, TILE)
-                grad[:, cols] = jnp.dot(acts_t[...], right, preferred_element_type=F32)
+                early = x_all[:c, :, :, cols].reshape(c * rows, TILE)
+                grad[:, cols] = jnp.dot(acts_t[...], right, preferred_element_type=F32) + jnp.dot(
+                    g_pre_t[:, :c * rows], early, preferred_element_type=F32
+                )
         stages[s](c)
     e_copy = copy(eb_sum.at[dat], eb_sum.at[dat], e_sem, {"dat": other})
     e_copy.start()
     for t in range(width // TILE):
         cols = slice(t * TILE, (t + 1) * TILE)
-        right = x_all[:, :, :, cols].reshape(CHUNKS * rows, TILE)
-        grown = grad[:, cols] + jnp.dot(g_pre_t[...], right, preferred_element_type=F32)
-        gw_ref[:, cols] = grown.astype(BF16)
+        right = x_all[CHUNKS - 1, :, :, cols].reshape(rows, TILE)
+        late = jnp.dot(g_pre_t[:, (CHUNKS - 1) * rows:], right, preferred_element_type=F32)
+        done[:, cols] = (grad[:, cols] + late).astype(BF16)
+        out_copy(t).start()
+    for t in range(width // TILE):
+        out_copy(t).wait()
     e_copy.wait()
     ge_ref[...] = eb_sum[...]
 
@@ -214,7 +236,6 @@
     half = inputs.shape[0] // CHUNKS
     rows, piece = 2 * half, half // n_lat
     whole = pl.BlockSpec(memory_space=pltpu.VMEM)
-    codes = jnp.swapaxes(row_code.reshape(2, CHUNKS, half), 0, 1).reshape(CHUNKS, rows, 1)
     pair = lambda v: v.reshape(2, 1, lats)
     sems = lambda *shape: pltpu.SemaphoreType.DMA(shape + (2,))
     grad_weight, grad_enc_bias, grad_dec_bias = pl.pallas_call(
@@ -222,10 +243,10 @@
         out_shape=(
             jax.ShapeDtypeStruct((lats, width), BF16),
             jax.ShapeDtypeStruct((2, 1, lats), F32),
-            jax.ShapeDtypeStruct((1, width), F32),
+            jax.ShapeDtypeStruct((width // LANES, LANES), F32),
         ),
         in_specs=[pl.BlockSpec(memory_space=pltpu.SMEM)] + [whole] * 7,
-        out_specs=(whole,) * 3,
+        out_specs=(pl.BlockSpec(memory_space=pl.ANY), whole, whole),
         scratch_shapes=[
             pltpu.VMEM((CHUNKS, 2, half, width), BF16),
             pltpu.VMEM((CHUNKS, rows, lats), BF16),
@@ -240,16 +261,18 @@
             pltpu.VMEM((CHUNKS, n_wid - 1, rows, lats), BF16),
             pltpu.VMEM((lats, CHUNKS * rows), BF16),
             pltpu.VMEM((lats, width), F32),
+            pltpu.VMEM((lats, width), BF16),
             pltpu.VMEM((2, 1, lats), F32),
             sems(CHUNKS), sems(CHUNKS, n_wid - 1), sems(CHUNKS), sems(CHUNKS, n_lat - 1),
             sems(CHUNKS, n_lat - 1), sems(CHUNKS), sems(CHUNKS, n_wid - 1), sems(),
+            pltpu.SemaphoreType.DMA((width // TILE,)),
         ],
         compiler_params=pltpu.CompilerParams(
             collective_id=0, has_side_effects=True, vmem_limit_bytes=56 * 1024 * 1024
         ),
     )(
         loss_scale, inputs.reshape(CHUNKS, half, width), weight, pair(enc_bias),
-        dec_bias.reshape(1, width), codes, pair(lat_code), pair(lat_thr),
+        dec_bias.reshape(width // LANES, LANES), row_code.reshape(1, -1), pair(lat_code), pair(lat_thr),
     )
     return (grad_weight, grad_enc_bias.reshape(-1), grad_dec_bias.reshape(-1))
 
@@ -258,7 +281,7 @@
     n_wid, n_lat = mesh.shape["wid"], mesh.shape["lat"]
     return (
         mesh.shape["dat"] == 2 and n_wid == 2 and 2 <= n_lat <= 8
-        and rows % (CHUNKS * n_lat * 16) == 0 and lats % TILE == 0 and width % TILE == 0
+        and rows % (CHUNKS * n_lat * 16) == 0 and lats % TILE == 0 and 2 * rows % (CHUNKS * LANES) == 0 and width % TILE == 0
         and lats * width <= 2 ** 21 and rows <= 256
     )
 

time: 92.1 us -> 84.2 us (0.914)
  Pallas kernels: 81.5 us -> 76.6 us
  local copies, waits for them, and re-layouts: 7.7 us -> 5.33 us
  other arithmetic: 1.31 us -> 0 us
    pallas_call x1, Pallas kernels: 81.5 us -> 76.6 us  [fused(): pl.pallas_call(functools.partial(kernel, n_wid, n_lat), out_shape=(jax.Sh...]
    reshape x3 -> x0, local copies, waits for them, and re-layouts: 2.97 us -> none  [the longest x1 1.29 us: fused(): dec_bias.reshape(1, width)]
    pallas_call x1 -> x0, other arithmetic: 1.31 us -> none  [fused(): pl.pallas_call(functools.partial(kernel, n_wid, n_lat), out_shape=(jax.Sh...]
    unnamed x4 -> x7, local copies, waits for them, and re-layouts: 4.73 us -> 5.33 us
where the time goes in v2:
time: 84.2 us; the launch traced here: 83.3 us
  Pallas kernels  76.6 us (91%)
  local copies, waits for them, and re-layouts  5.33 us (6%)
  between operations  1.31 us (2%)
    pallas_call x1, Pallas kernels, fused(): pl.pallas_call(functools.partial(kernel, n_wid, n_lat), out_shape=(jax.Sh...  76.6 us
    unnamed x7, local copies, waits for them, and re-layouts  5.33 us

profile of v2, /device:TPU:0, one launch (start us, length us, event | category | flops | bytes accessed | tf_op | source)
XLA Modules:
  0.0 83.3 jit_solution(914471585144001431)
XLA Ops:
  1.3 76.6 %shard_map.103 = (bf16[1024,1792]{1,0:T(8,128)(2,1)}, f32[2,1,1024]{2,1,0:T(1,128)}, f32[14,128]{1,0:T(8,128)}) custom-call(f32[1]{0:T(128)S(6)} %copy.14.scale_ref, bf16[4,64,1792]{2,1,0:T(8,128)(2,1)} %bitcast.8, bf16[1024,1792]{1,0:T(8,128)(2,1)} %w_ref.1, f32[2,1,1024]{2,1,0:T(1,128)} %bitcast.9, f32[14,128]{1,0:T(8,128)} %bitcast.10, ...), custom_call_target="tpu_custom_call" | custom-call | tf_op jit(solution)/shard_map/pallas_call | solution.py:241
  77.9 0.0 copy-start.1
  77.9 0.0 copy-start
  77.9 4.1 %copy.15 = bf16[1024,1792]{1,0:T(8,128)(2,1)} copy(bf16[1024,1792]{1,0:T(8,128)(2,1)} %get-tuple-element.12) | data formatting | bytes 7340032
  82.0 0.0 copy-done.1
  82.0 0.6 copy.16
  82.6 0.0 copy-done
  82.7 0.6 copy.17
Async XLA Ops:
  77.9 4.1 %copy-start.1 = (f32[2,1,1024]{2,1,0:T(1,128)S(1)}, f32[2,1,1024]{2,1,0:T(1,128)}, u32[]{:S(2)}) copy-start(f32[2,1,1024]{2,1,0:T(1,128)} %get-tuple-element.7) | copy-start | bytes 24580
  77.9 4.7 %copy-start = (f32[14,128]{1,0:T(8,128)S(1)}, f32[14,128]{1,0:T(8,128)}, u32[]{:S(2)}) copy-start(f32[14,128]{1,0:T(8,128)} %get-tuple-element.8) | copy-start | bytes 21508

commit v3 on v2

--- a/solution.py
+++ b/solution.py
@@ -13,8 +13,8 @@
 CHUNKS = 4
 TILE = 256
 LANES = 128
-STAGE_AT = (0, 10, 15, 30, 45, 48, 60)
-CHUNK_STEP = 10
+STAGE_AT = (0, 10, 15, 21, 29, 37, 40, 52)
+CHUNK_STEP = 8
 
 
 def times_rows(left, right):
@@ -57,8 +57,8 @@
 def kernel(
     n_wid, n_lat, scale_ref, x_ref, w_ref, eb_ref, db_ref, rc_ref, lc_ref, thr_ref,
     gw_ref, ge_ref, gd_ref,
-    x_all, p_out, p_in, acts_t, rec, rec_in, summed, pieces, g_all, q_out, q_in, g_pre_t, grad, done, eb_sum,
-    x_sem, p_sem, c_sem, s_sem, a_sem, h_sem, q_sem, e_sem, w_sem,
+    x_all, p_out, p_in, acts_t, rec, rec_in, summed, near_in, paired, far_in, g_all, q_out, q_in, g_pre_t, grad, done, eb_sum,
+    x_sem, p_sem, c_sem, s_sem, f_sem, a_sem, h_sem, q_sem, e_sem, w_sem,
 ):
     wid, lat, dat = lax.axis_index("wid"), lax.axis_index("lat"), lax.axis_index("dat")
     other = 1 - dat
@@ -66,10 +66,11 @@
     lats = w_ref.shape[0]
     rows = 2 * half
     wid_peers = [lax.rem(wid + k, n_wid) for k in range(1, n_wid)]
-    lat_peers = [lax.rem(lat + k, n_lat) for k in range(1, n_lat)]
+    side = lax.rem(lat, 2)
+    near, far = lat + 1 - 2 * side, lax.rem(lat + 2, n_lat)
 
     barrier = pltpu.get_barrier_semaphore()
-    everyone = [{"dat": other}] + [{"wid": p} for p in wid_peers] + [{"lat": p} for p in lat_peers]
+    everyone = [{"dat": other}] + [{"wid": p} for p in wid_peers] + [{"lat": near}, {"lat": far}]
     for peer in everyone:
         pl.semaphore_signal(barrier, inc=1, device_id=peer, device_id_type=MESH)
     pl.semaphore_wait(barrier, len(everyone))
@@ -92,14 +93,14 @@
     def c_copy(c):
         return copy(rec.at[c, other], rec_in.at[c], c_sem.at[c], {"dat": other})
 
-    def s_copies(c):
-        return [copy(summed.at[c, p], pieces.at[c, k], s_sem.at[c, k], {"lat": p}) for k, p in enumerate(lat_peers)]
-
-    def a_copies(c):
-        return [
-            copy(g_all.at[c, dat, lat], g_all.at[c, dat, lat], a_sem.at[c, k], {"lat": p})
-            for k, p in enumerate(lat_peers)
-        ]
+    def s_copy(c):
+        return copy(summed.at[c, 1 - side], near_in.at[c], s_sem.at[c], {"lat": near})
+
+    def f_copy(c):
+        return copy(paired.at[c], far_in.at[c], f_sem.at[c], {"lat": far})
+
+    def a_copy(c):
+        return copy(g_all.at[c, dat, side], g_all.at[c, dat, side], a_sem.at[c], {"lat": near})
 
     def h_copy(c):
         return copy(g_all.at[c, dat], g_all.at[c, dat], h_sem.at[c], {"dat": other})
@@ -150,31 +151,30 @@
         c_copy(c).wait()
         both = rec[c, dat].astype(F32) + rec_in[c].astype(F32)
         summed[c] = both.astype(BF16).reshape(summed.shape[1:])
-        for one in s_copies(c):
-            one.start()
+        s_copy(c).start()
+
+    def near_sum(c):
+        s_copy(c).wait()
+        paired[c] = (summed[c, side].astype(F32) + near_in[c].astype(F32)).astype(BF16)
+        f_copy(c).start()
 
     def gradient(c):
-        for one in s_copies(c):
-            one.wait()
-        recon = summed[c, lat].astype(F32)
-        for k in range(n_lat - 1):
-            recon = recon + pieces[c, k].astype(F32)
+        f_copy(c).wait()
+        recon = paired[c].astype(F32) + far_in[c].astype(F32)
         own = x_piece(c)
         g_rec = scale_ref[0] * (2.0 / (rows * CHUNKS)) * (recon + bias_row() - own.astype(F32))
-        g_all[c, dat, lat] = g_rec.astype(BF16)
-        for one in a_copies(c):
-            one.start()
+        g_all[c, dat, side] = g_rec.astype(BF16)
+        a_copy(c).start()
 
     def bias_row():
         return jnp.concatenate([db_ref[i:i + 1, :] for i in range(width // LANES)], axis=1)
 
     def x_piece(c):
-        count = half // n_lat
-        return x_ref[c, pl.ds(pl.multiple_of(lat * count, count), count), :]
+        count = half // 2
+        return x_ref[c, pl.ds(pl.multiple_of(side * count, count), count), :]
 
     def share(c):
-        for one in a_copies(c):
-            one.wait()
+        a_copy(c).wait()
         h_copy(c).start()
 
     def back(c):
@@ -203,7 +203,7 @@
     for c in range(CHUNKS):
         x_copy(c).start()
     x_all[:, dat] = x_ref[...]
-    stages = (encode, decode, core_sum, gradient, share, back, gate)
+    stages = (encode, decode, core_sum, near_sum, gradient, share, back, gate)
     order = sorted(
         (STAGE_AT[s] + (CHUNK_STEP if s else 1) * c, s, c) for s in range(len(stages)) for c in range(CHUNKS)
     )
@@ -234,7 +234,7 @@
 def fused(n_wid, n_lat, inputs, weight, enc_bias, dec_bias, row_code, lat_code, lat_thr, loss_scale):
     lats, width = weight.shape
     half = inputs.shape[0] // CHUNKS
-    rows, piece = 2 * half, half // n_lat
+    rows, piece = 2 * half, half // 2
     whole = pl.BlockSpec(memory_space=pltpu.VMEM)
     pair = lambda v: v.reshape(2, 1, lats)
     sems = lambda *shape: pltpu.SemaphoreType.DMA(shape + (2,))
@@ -254,17 +254,19 @@
             pltpu.VMEM((lats, CHUNKS * rows), BF16),
             pltpu.VMEM((CHUNKS, 2, half, width), BF16),
             pltpu.VMEM((CHUNKS, half, width), BF16),
-            pltpu.VMEM((CHUNKS, n_lat, piece, width), BF16),
-            pltpu.VMEM((CHUNKS, n_lat - 1, piece, width), BF16),
-            pltpu.VMEM((CHUNKS, 2, n_lat, piece, width), BF16),
+            pltpu.VMEM((CHUNKS, 2, piece, width), BF16),
+            pltpu.VMEM((CHUNKS, piece, width), BF16),
+            pltpu.VMEM((CHUNKS, piece, width), BF16),
+            pltpu.VMEM((CHUNKS, piece, width), BF16),
+            pltpu.VMEM((CHUNKS, 2, 2, piece, width), BF16),
             pltpu.VMEM((CHUNKS, rows, lats), BF16),
             pltpu.VMEM((CHUNKS, n_wid - 1, rows, lats), BF16),
             pltpu.VMEM((lats, CHUNKS * rows), BF16),
             pltpu.VMEM((lats, width), F32),
             pltpu.VMEM((lats, width), BF16),
             pltpu.VMEM((2, 1, lats), F32),
-            sems(CHUNKS), sems(CHUNKS, n_wid - 1), sems(CHUNKS), sems(CHUNKS, n_lat - 1),
-            sems(CHUNKS, n_lat - 1), sems(CHUNKS), sems(CHUNKS, n_wid - 1), sems(),
+            sems(CHUNKS), sems(CHUNKS, n_wid - 1), sems(CHUNKS), sems(CHUNKS),
+            sems(CHUNKS), sems(CHUNKS), sems(CHUNKS), sems(CHUNKS, n_wid - 1), sems(),
             pltpu.SemaphoreType.DMA((width // TILE,)),
         ],
         compiler_params=pltpu.CompilerParams(
@@ -280,8 +282,8 @@
 def fits(mesh, rows, lats, width):
     n_wid, n_lat = mesh.shape["wid"], mesh.shape["lat"]
     return (
-        mesh.shape["dat"] == 2 and n_wid == 2 and 2 <= n_lat <= 8
-        and rows % (CHUNKS * n_lat * 16) == 0 and lats % TILE == 0 and 2 * rows % (CHUNKS * LANES) == 0 and width % TILE == 0
+        mesh.shape["dat"] == 2 and n_wid == 2 and n_lat == 4
+        and rows % (CHUNKS * 2 * 16) == 0 and lats % TILE == 0 and 2 * rows % (CHUNKS * LANES) == 0 and width % TILE == 0
         and lats * width <= 2 ** 21 and rows <= 256
     )
 

time: 84.2 us -> 81.8 us (0.971)
  Pallas kernels: 76.6 us -> 75 us
    pallas_call x1, Pallas kernels: 76.6 us -> 75 us  [fused(): pl.pallas_call(functools.partial(kernel, n_wid, n_lat), out_shape=(jax.Sh...]
where the time goes in v3:
time: 81.8 us; the launch traced here: 81.6 us
  Pallas kernels  75 us (92%)
  local copies, waits for them, and re-layouts  5.33 us (7%)
  between operations  1.31 us (2%)
    pallas_call x1, Pallas kernels, fused(): pl.pallas_call(functools.partial(kernel, n_wid, n_lat), out_shape=(jax.Sh...  75 us
    unnamed x7, local copies, waits for them, and re-layouts  5.33 us

profile of v3, /device:TPU:0, one launch (start us, length us, event | category | flops | bytes accessed | tf_op | source)
XLA Modules:
  0.0 81.6 jit_solution(14055727844138083207)
XLA Ops:
  1.3 75.0 %shard_map.103 = (bf16[1024,1792]{1,0:T(8,128)(2,1)}, f32[2,1,1024]{2,1,0:T(1,128)}, f32[14,128]{1,0:T(8,128)}) custom-call(f32[1]{0:T(128)S(6)} %copy.14.scale_ref, bf16[4,64,1792]{2,1,0:T(8,128)(2,1)} %bitcast.8, bf16[1024,1792]{1,0:T(8,128)(2,1)} %w_ref.1, f32[2,1,1024]{2,1,0:T(1,128)} %bitcast.9, f32[14,128]{1,0:T(8,128)} %bitcast.10, ...), custom_call_target="tpu_custom_call" | custom-call | tf_op jit(solution)/shard_map/pallas_call | solution.py:241
  76.3 0.0 copy-start.1
  76.3 0.0 copy-start
  76.3 4.1 %copy.15 = bf16[1024,1792]{1,0:T(8,128)(2,1)} copy(bf16[1024,1792]{1,0:T(8,128)(2,1)} %get-tuple-element.12) | data formatting | bytes 7340032
  80.4 0.0 copy-done.1
  80.4 0.6 copy.16
  81.0 0.0 copy-done
  81.0 0.6 copy.17
Async XLA Ops:
  76.3 4.1 %copy-start.1 = (f32[2,1,1024]{2,1,0:T(1,128)S(1)}, f32[2,1,1024]{2,1,0:T(1,128)}, u32[]{:S(2)}) copy-start(f32[2,1,1024]{2,1,0:T(1,128)} %get-tuple-element.7) | copy-start | bytes 24580
  76.3 4.7 %copy-start = (f32[14,128]{1,0:T(8,128)S(1)}, f32[14,128]{1,0:T(8,128)}, u32[]{:S(2)}) copy-start(f32[14,128]{1,0:T(8,128)} %get-tuple-element.8) | copy-start | bytes 21508
